TPU v7x, 32 devices: a whole 2x2x4 slice. The times are simulated.
32 devices in a mesh: cells: 8 (over z, y), spec: 4 (over x, core).
Axes of the slice: x: 2, y: 2, z: 4, core: 2. Of those that a mesh axis runs over, the one named last changes fastest.
Arguments:
- wind_field: float32 [2, 16, 16384], P(None, 'spec', 'cells'), may hold values from -6 to 6
- damping: float32 [16], P('spec'), may hold values from 0.002 to 0.02
- atm_table: int32 [3, 16384], P(None, 'cells'), may hold values from 0 to 3071, as said below
- atm_coef: float32 [3, 16384], P(None, 'cells'), may hold values from 0.5 to 1.5
- atm_send: int32 [8192], P('cells'), may hold values from 0 to 2047
- send_cells: int32 [64, 256], P('cells'), may hold values from 0 to 2047
- block_count: int32 [64], P('cells'), may hold values from 1 to 256, as said below
- slot_weight: float32 [64, 256], P('cells'), may hold values from 0.05 to 0.4
- recv_cells: int32 [64, 256], P('cells'), may hold values from 0 to 511
- spectra: float32 [36, 12, 4096], P(None, 'spec', 'cells'), may hold values from 0.005 to 16, as said below
- sea_mask: int32 [4096], P('cells'), may hold values 0 or 1
- ocn_table: int32 [3, 4096], P(None, 'cells'), may hold values from 0 to 767, as said below
- face_angle: float32 [3, 4096], P(None, 'cells'), may hold values from -3.140625 to 3.140625
- face_ratio: float32 [3, 4096], P(None, 'cells'), may hold values from 0.1 to 0.35
- ocn_send: int32 [2048], P('cells'), may hold values from 0 to 511
Outputs:
- wind_out: float32 [2, 16, 16384], P(None, 'spec', 'cells')
- spectra_new: float32 [36, 12, 4096], P(None, 'spec', 'cells')
Inputs may be any that keep to these rules, and one draw needn't show every extreme that they name: `atm_table`: each own cell's entries point into its device's extended patch, within 512 positions of the cell's own place. `ocn_table`: each own cell's entries point into its device's extended patch, within 128 positions of the cell's own place. `block_count`: some ocean device receives 256 live slots from every atmosphere device. `spectra`: positive.
All inputs are finite; a program needn't handle non-finite values. No bound on the sum of `sea_mask` on one device may be relied on, other than what follows from the above.
Results may differ from a plain program's by a relative error of at most 0.00002.
Values sent between devices are 32-bit elements; how exact they have to be, the bound alone decides.
A program may use at most 64 MiB of HBM per device.

v0:
```python
import math

import jax
import jax.numpy as jnp
from jax import lax
from jax.sharding import PartitionSpec as P

DIRECTIONS = 36
BANDS = 12


epsilon = 1e-06
wind_factor = 0.8
growth = 0.1
coupling = 4.0
dissipation = 0.05


def padded(block, sides, width):
    for axis, dim in sides:
        count = lax.axis_size(axis)
        forward = [(i, i + 1) for i in range(count - 1)]
        forward.append((count - 1, 0))
        backward = [(target, source) for source, target in forward]
        low = lax.ppermute(
            lax.slice_in_dim(block, block.shape[dim] - width, None, axis=dim), axis, forward
        )
        high = lax.ppermute(lax.slice_in_dim(block, 0, width, axis=dim), axis, backward)
        block = jnp.concatenate([low, block, high], axis=dim)
    return block


def spread(value, axis, source):
    kept = jnp.where(lax.axis_index(axis) == source, value, 0).astype(value.dtype)
    return lax.psum(kept, axis)


def laplace_cells(extended, fields, neighbours, lap_weight):
    gathered = extended[:, neighbours]
    return jnp.sum(lap_weight[None] * (gathered - fields[:, None, :]), axis=1)


def atm_laplace(fields, send_list, neighbours, lap_weight):
    rim_width = send_list.shape[0] // 2
    grown = padded(fields[:, send_list], (("cells", 1),), rim_width)
    extended = jnp.concatenate([grown[:, :rim_width], fields, grown[:, 3 * rim_width :]], axis=1)
    return laplace_cells(extended, fields, neighbours, lap_weight)


def pack_blocks(surface, cell_slots, counts, weights):
    slot_index = jnp.arange(cell_slots.shape[1], dtype=jnp.int32)
    active = slot_index[None, :] < counts[:, None]
    slot_scale = jnp.where(active, weights, 0.0)
    return surface[:, cell_slots] * slot_scale[None]


def band_terms(energy, frequency):
    component_count = DIRECTIONS * BANDS
    mean_energy = jnp.sum(energy, axis=(0, 1)) / component_count
    inverse = jnp.sum(energy / frequency[None, :, None], axis=(0, 1)) / component_count
    return (mean_energy, inverse)


def sources(energy, wind, mean_energy, inverse, frequency, heading):
    wind_along = (
        jnp.cos(heading)[:, None] * wind[0][None] + jnp.sin(heading)[:, None] * wind[1][None]
    )
    gain_in = (
        growth
        * frequency[None, :, None]
        * jnp.maximum(coupling * frequency[None, :, None] * wind_along[:, None, :] - 1.0, 0.0)
    )
    mean_freq = mean_energy / (inverse + epsilon)
    decay_rate = (
        dissipation * frequency[None, :, None] * (mean_energy * mean_freq**4)[None, None, :]
    )
    return energy * (1.0 + gain_in) / (1.0 + decay_rate)


def propagate(energy, extended, neighbours, phase, ratio, group_speed, heading):
    result = energy
    for border in range(3):
        normal = (
            jnp.cos(heading)[:, None] * jnp.cos(phase[border])[None]
            + jnp.sin(heading)[:, None] * jnp.sin(phase[border])[None]
        )
        transport = group_speed[None, :, None] * normal[:, None, :] * ratio[border][None, None, :]
        upwind = extended[:, :, neighbours[border]]
        result = result - (
            jnp.maximum(transport, 0.0) * energy + jnp.minimum(transport, 0.0) * upwind
        )
    return result


def local(
    wind_field,
    damping,
    atm_table,
    atm_coef,
    atm_send,
    send_cells,
    block_count,
    slot_weight,
    recv_cells,
    spectra,
    sea_mask,
    ocn_table,
    face_angle,
    face_ratio,
    ocn_send,
):
    level_dev = wind_field.shape[1]
    fields = wind_field.reshape(2 * level_dev, -1)
    lap_once = atm_laplace(fields, atm_send, atm_table, atm_coef)
    lap_twice = atm_laplace(lap_once, atm_send, atm_table, atm_coef)
    damp_rate = jnp.concatenate([damping, damping])[:, None]
    damped = fields - damp_rate * lap_twice
    wind_out = damped.reshape(wind_field.shape)
    spec_count = lax.axis_size("spec")
    surface = wind_factor * damped.reshape(2, level_dev, -1)[:, level_dev - 1]
    surface = spread(surface, "spec", spec_count - 1)
    ocean_count = spectra.shape[2]
    blocks = pack_blocks(surface, send_cells, block_count, slot_weight)
    arrived = lax.all_to_all(blocks, "cells", split_axis=1, concat_axis=1, tiled=True)
    flat_places = recv_cells.reshape(-1)
    ocean_wind = (
        jnp.zeros((2, ocean_count), jnp.float32).at[:, flat_places].add(arrived.reshape(2, -1))
    )
    bands_dev = spectra.shape[1]
    band_index = lax.axis_index("spec") * bands_dev + jnp.arange(bands_dev, dtype=jnp.int32)
    frequency = 0.6 * 1.1 ** band_index.astype(jnp.float32)
    group_speed = 0.5 / frequency
    heading = (jnp.arange(DIRECTIONS, dtype=jnp.float32) + 0.5) * (2.0 * math.pi / DIRECTIONS)
    energy = spectra * sea_mask.astype(jnp.float32)[None, None, :]
    rim_width = ocn_send.shape[0] // 2
    own_total, own_inverse = band_terms(energy, frequency)
    mean_energy, inverse = lax.psum((own_total, own_inverse), "spec")
    updated = sources(energy, ocean_wind, mean_energy, inverse, frequency, heading)
    flat = updated.reshape(-1, ocean_count)
    grown = padded(flat[:, ocn_send], (("cells", 1),), rim_width)
    extended = jnp.concatenate([grown[:, :rim_width], flat, grown[:, 3 * rim_width :]], axis=1)
    extended = extended.reshape(DIRECTIONS, bands_dev, -1)
    spectra_new = propagate(
        updated, extended, ocn_table, face_angle, face_ratio, group_speed, heading
    )
    return (wind_out, spectra_new)


def solution(mesh):
    in_specs = (
        P(None, "spec", "cells"),
        P("spec"),
        P(None, "cells"),
        P(None, "cells"),
        P("cells"),
        P("cells", None),
        P("cells"),
        P("cells", None),
        P("cells", None),
        P(None, "spec", "cells"),
        P("cells"),
        P(None, "cells"),
        P(None, "cells"),
        P(None, "cells"),
        P("cells"),
    )
    out_specs = (P(None, "spec", "cells"), P(None, "spec", "cells"))
    return jax.shard_map(local, mesh=mesh, in_specs=in_specs, out_specs=out_specs, check_vma=False)
```

profile of v0, /device:TPU:0, one launch (start us, length us, event | category | flops | bytes accessed | tf_op | source)
XLA Modules:
  0.0 174.0 jit_solution(583655927343548966)
XLA Ops:
  0.6 0.9 reshape.418
  1.5 0.3 copy.113
  1.9 0.7 fusion.12
  2.6 2.8 %gather_fusion = f32[1024,8]{1,0:T(8,128)S(1)} fusion(f32[8,2048]{0,1:T(8,128)S(1)} %copy.113, s32[1024]{0:T(1024)S(1)} %fusion.12), kind=kCustom, calls=%fused_computation | custom fusion | bytes 69632 | tf_op jit(solution)/shard_map/gather | solution.py:45
  5.4 3.0 %collective-permute-start = (f32[8,512]{0,1:T(8,128)S(1)}, f32[8,512]{0,1:T(8,128)S(1)}, u32[]{:S(2)}, u32[]{:S(2)}) collective-permute-start(f32[8,512]{0,1:T(8,128)S(1)} %get-tuple-element.23), channel_id=1, source_target_pairs={{0,4},{4,8},{8,12},{12,16},{16,20},{20,24},{24,28},{28,0},{1,5},{5... | collective-permute-start | bytes 49160 | tf_op jit(solution)/shard_map/ppermute | solution.py:25
  8.5 3.1 %collective-permute-start.1 = (f32[8,512]{0,1:T(8,128)S(1)}, f32[8,512]{0,1:T(8,128)S(1)}, u32[]{:S(2)}, u32[]{:S(2)}) collective-permute-start(f32[8,512]{0,1:T(8,128)S(1)} %get-tuple-element.24), channel_id=1, source_target_pairs={{4,0},{8,4},{12,8},{16,12},{20,16},{24,20},{28,24},{0,28},{5,1},{9... | collective-permute-start | bytes 49160 | tf_op jit(solution)/shard_map/ppermute | solution.py:28
  11.6 0.6 broadcast_divide_fusion
  12.2 0.8 compare_select_fusion
  13.0 0.7 convert_element_type.24
  13.7 0.7 fusion.10
  14.4 0.7 copy.134
  15.1 1.0 slice_cosine_fusion.2
  16.1 0.7 compare_select_fusion.7
  16.8 0.8 compare_select_fusion.5
  17.7 0.8 fusion.18
  18.5 1.1 divide_reduce_fusion
  19.7 2.2 %collective-permute-done.1 = f32[8,512]{0,1:T(8,128)S(1)} collective-permute-done((f32[8,512]{0,1:T(8,128)S(1)}, f32[8,512]{0,1:T(8,128)S(1)}, u32[]{:S(2)}, u32[]{:S(2)}) %collective-permute-start.1) | collective-permute-done | bytes 16416 | tf_op jit(solution)/shard_map/ppermute | solution.py:28
  21.8 1.3 pad_maximum_fusion
  23.1 22.5 %gather_fusion.1 = f32[6144,8]{1,0:T(8,128)} fusion(f32[8,3072]{0,1:T(8,128)} %pad_maximum_fusion, s32[6144]{0:T(1024)S(1)} %broadcast_clamp_fusion), kind=kCustom, calls=%fused_computation.1 | custom fusion | bytes 417792 | tf_op jit(solution)/shard_map/gather | solution.py:39
  45.6 2.5 %multiply_reduce_fusion.1 = f32[8,2048]{0,1:T(8,128)S(1)} fusion(f32[8,3,2048]{0,2,1:T(8,128)} %bitcast.66, f32[8,2048]{0,1:T(8,128)S(1)} %copy.113, f32[3,2048]{1,0:T(4,128)S(1)} %copy-done.3), kind=kLoop, calls=%fused_computation.12 | loop fusion | flops 131072 | bytes 352256 | tf_op jit(solution)/shard_map/reduce_sum | solution.py:40
  48.0 2.8 %gather_fusion.2 = f32[1024,8]{1,0:T(8,128)S(1)} fusion(f32[8,2048]{0,1:T(8,128)S(1)} %multiply_reduce_fusion.1, s32[1024]{0:T(1024)S(1)} %fusion.12), kind=kCustom, calls=%fused_computation.2 | custom fusion | bytes 69632 | tf_op jit(solution)/shard_map/gather | solution.py:45
  50.9 0.3 collective-permute-start.2
  51.2 4.4 %collective-permute-start.3 = (f32[8,512]{0,1:T(8,128)S(1)}, f32[8,512]{0,1:T(8,128)S(1)}, u32[]{:S(2)}, u32[]{:S(2)}) collective-permute-start(f32[8,512]{0,1:T(8,128)S(1)} %get-tuple-element.22), channel_id=1, source_target_pairs={{4,0},{8,4},{12,8},{16,12},{20,16},{24,20},{28,24},{0,28},{5,1},{9... | collective-permute-start | bytes 49160 | tf_op jit(solution)/shard_map/ppermute | solution.py:28
  55.7 2.6 %copy.118 = f32[2,4,2048]{0,2,1:T(8,128)} copy(f32[2,4,2048]{2,1,0:T(4,128)S(1)} %copy-done.2) | data formatting | bytes 131072 | tf_op args[0]
  58.5 3.0 %collective-permute-done.2 = f32[8,512]{0,1:T(8,128)S(1)} collective-permute-done((f32[8,512]{0,1:T(8,128)S(1)}, f32[8,512]{0,1:T(8,128)S(1)}, u32[]{:S(2)}, u32[]{:S(2)}) %collective-permute-start.2) | collective-permute-done | bytes 16416 | tf_op jit(solution)/shard_map/ppermute | solution.py:25
  61.5 3.9 %collective-permute-done.3 = f32[8,512]{0,1:T(8,128)S(1)} collective-permute-done((f32[8,512]{0,1:T(8,128)S(1)}, f32[8,512]{0,1:T(8,128)S(1)}, u32[]{:S(2)}, u32[]{:S(2)}) %collective-permute-start.3) | collective-permute-done | bytes 16416 | tf_op jit(solution)/shard_map/ppermute | solution.py:28
  65.6 21.0 %gather_fusion.3 = f32[6144,8]{1,0:T(8,128)} fusion(f32[8,3072]{0,1:T(8,128)S(1)} %pad_maximum_fusion.1, s32[6144]{0:T(1024)S(1)} %broadcast_clamp_fusion), kind=kCustom, calls=%fused_computation.3 | custom fusion | bytes 417792 | tf_op jit(solution)/shard_map/gather | solution.py:39
  86.6 2.5 %multiply_reduce_fusion = f32[8,2048]{0,1:T(8,128)S(1)} fusion(f32[8,3,2048]{0,2,1:T(8,128)} %bitcast.65, f32[8,2048]{0,1:T(8,128)S(1)} %multiply_reduce_fusion.1, f32[3,2048]{1,0:T(4,128)S(1)} %copy-done.3), kind=kLoop, calls=%fused_computation.11 | loop fusion | flops 131072 | bytes 352256 | tf_op jit(solution)/shard_map/reduce_sum | solution.py:40
  89.4 2.7 %copy.117 = f32[2,4,2048]{0,2,1:T(8,128)} copy(f32[2,4,2048]{2,1,0:T(4,128)S(1)} %reduce_sum.40) | data formatting | bytes 131072 | tf_op jit(solution)/shard_map/reduce_sum | solution.py:40
  92.1 3.9 %multiply_subtract_fusion = f32[2,4,2048]{0,2,1:T(8,128)S(1)} fusion(f32[2,4,2048]{0,2,1:T(8,128)} %copy.118, f32[2,4,2048]{0,2,1:T(8,128)} %copy.117, f32[2,4]{0,1:T(4,128)S(1)} %copy.112), kind=kLoop, calls=%fused_computation.10 | loop fusion | flops 32768 | bytes 196640 | tf_op jit(solution)/shard_map/sub | solution.py:117
  96.0 1.9 %copy-done = f32[2,4,2048]{0,2,1:T(8,128)} copy-done((f32[2,4,2048]{0,2,1:T(8,128)}, f32[2,4,2048]{0,2,1:T(8,128)S(1)}, u32[]{:S(2)}) %copy-start) | copy-done | bytes 65560
  98.0 26.0 %all-reduce = (f32[512]{0:T(512)S(1)}, f32[512]{0:T(512)S(1)}, f32[2,2048]{0,1:T(8,128)S(1)}) all-reduce(f32[512]{0:T(512)S(1)} %get-tuple-element.48, f32[512]{0:T(512)S(1)} %get-tuple-element.47, f32[2,2048]{0,1:T(8,128)S(1)} %fusion.1), channel_id=1, replica_groups=mesh['cells'=8,'spec'=4] {'spec'}, use_global_device_ids=true, to_apply=%region_5.6 | all-reduce | flops 5120 | bytes 40960 | tf_op jit(solution)/shard_map/psum | solution.py:137
  124.0 5.5 %gather_fusion.4 = f32[2048,2]{1,0:T(8,128)S(1)} fusion(f32[2,2048]{0,1:T(8,128)S(1)} %get-tuple-element.20, s32[2048]{0:T(1024)S(1)} %broadcast_clamp_fusion.1), kind=kCustom, calls=%fused_computation.4 | custom fusion | bytes 40960 | tf_op jit(solution)/shard_map/gather | solution.py:54
  129.8 0.6 multiply_bitcast_fusion
  130.4 4.3 %all-to-all-start = ((f32[2,8,256]{2,0,1:T(2,128)}), f32[2,8,256]{2,0,1:T(2,128)S(1)}, u32[]{:S(2)}, u32[]{:S(2)}) async-start(f32[2,8,256]{2,0,1:T(2,128)} %multiply_bitcast_fusion), calls=%async_computation | async-start | bytes 32768 | tf_op jit(solution)/shard_map/all_to_all | solution.py:124
  134.8 6.5 %all-to-all-done = f32[2,8,256]{2,0,1:T(2,128)S(1)} async-done(((f32[2,8,256]{2,0,1:T(2,128)}), f32[2,8,256]{2,0,1:T(2,128)S(1)}, u32[]{:S(2)}, u32[]{:S(2)}) %all-to-all-start) | async-done | bytes 16416 | tf_op jit(solution)/shard_map/all_to_all | solution.py:124
  141.3 0.4 copy.120
  141.6 11.5 %scatter_custom_fusion = f32[2,512]{0,1:T(8,128)S(1)} fusion(s32[2048]{0:T(1024)S(1)} %bitcast.84, f32[2048,2]{1,0:T(8,128)S(1)} %copy.120, f32[]{:T(128)} %constant.23.clone.1), kind=kCustom, calls=%fused_computation.33 | custom fusion | flops 4096 | bytes 4100 | tf_op jit(solution)/shard_map/scatter-add | solution.py:127
  153.5 0.8 multiply_add_fusion.2
  154.8 0.7 gather_fusion.5
  155.6 0.6 collective-permute-start.4
  156.1 4.2 %collective-permute-start.5 = (f32[108,128]{0,1:T(8,128)S(1)}, f32[108,128]{0,1:T(8,128)S(1)}, u32[]{:S(2)}, u32[]{:S(2)}) collective-permute-start(f32[108,128]{0,1:T(8,128)S(1)} %get-tuple-element.26), channel_id=1, source_target_pairs={{4,0},{8,4},{12,8},{16,12},{20,16},{24,20},{28,24},{0,28},{5,1},{9... | collective-permute-start | bytes 165896 | tf_op jit(solution)/shard_map/ppermute | solution.py:28
  160.3 3.5 %copy.133 = f32[2,4,2048]{2,1,0:T(4,128)} copy(f32[2,4,2048]{0,2,1:T(8,128)} %copy-done) | data formatting | bytes 131072
  164.2 0.7 copy.127
  164.9 2.1 %gather_fusion.6 = f32[512,36,3]{1,2,0:T(4,128)S(1)} fusion(f32[36,3,768]{0,1,2:T(4,128)S(1)} %copy.127, s32[1024]{0:T(1024)S(1)} %pad_clamp_fusion.2), kind=kCustom, calls=%fused_computation.6 | custom fusion | bytes 444416 | tf_op jit(solution)/shard_map/gather | solution.py:88
  167.3 2.1 %gather_fusion.7 = f32[512,36,3]{1,2,0:T(4,128)S(1)} fusion(f32[36,3,768]{0,1,2:T(4,128)S(1)} %copy.127, s32[1024]{0:T(1024)S(1)} %pad_clamp_fusion.1), kind=kCustom, calls=%fused_computation.7 | custom fusion | bytes 444416 | tf_op jit(solution)/shard_map/gather | solution.py:88
  169.7 2.1 %gather_fusion.8 = f32[512,36,3]{1,2,0:T(4,128)S(1)} fusion(f32[36,3,768]{0,1,2:T(4,128)S(1)} %copy.127, s32[1024]{0:T(1024)S(1)} %pad_clamp_fusion), kind=kCustom, calls=%fused_computation.8 | custom fusion | bytes 444416 | tf_op jit(solution)/shard_map/gather | solution.py:88
  172.1 2.0 %fusion.3 = f32[36,3,512]{2,0,1:T(8,128)} fusion(f32[512,36,3]{0,1,2:T(8,128)S(1)} %copy.132, f32[512,36,3]{0,1,2:T(8,128)S(1)} %copy.130, f32[512,36,3]{0,1,2:T(8,128)S(1)} %copy.128, f32[512]{0:T(512)S(1)} %bitcast.81, f32[36,512]{1,0:T(8,128)} %get-tuple-element.41, f32[512]{0:T(512)S(1)} %bitcast.82, f32[36,512]{1,0:T(8,128)} %get-tuple-element.40, ...), kind=kLoop, calls=%fused_computation.23 | loop fusion | flops 1769472 | bytes 1415204 | tf_op jit(solution)/shard_map/sub | solution.py:89
  (60 shorter events, 3.6 us)
Async XLA Ops:
  0.6 18.9 %copy-start.6 = (s32[8]{0:T(128)S(1)}, s32[8]{0:T(128)}, u32[]{:S(2)}) copy-start(s32[8]{0:T(128)} %param.21) | copy-start | bytes 100
  0.6 18.9 %copy-start.4 = (f32[8,256]{1,0:T(8,128)S(1)}, f32[8,256]{1,0:T(8,128)}, u32[]{:S(2)}) copy-start(f32[8,256]{1,0:T(8,128)} %param.22) | copy-start | bytes 24580
  5.4 40.1 %copy-start.3 = (f32[3,2048]{1,0:T(4,128)S(1)}, f32[3,2048]{1,0:T(4,128)}, u32[]{:S(2)}) copy-start(f32[3,2048]{1,0:T(4,128)} %param.18) | copy-start | bytes 73732
  5.4 14.2 %collective-permute-start = (f32[8,512]{0,1:T(8,128)S(1)}, f32[8,512]{0,1:T(8,128)S(1)}, u32[]{:S(2)}, u32[]{:S(2)}) collective-permute-start(f32[8,512]{0,1:T(8,128)S(1)} %get-tuple-element.23), channel_id=1, source_target_pairs={{0,4},{4,8},{8,12},{12,16},{16,20},{20,24},{24,28},{28,0},{1,5},{5... | collective-permute-start | bytes 49160 | tf_op jit(solution)/shard_map/ppermute | solution.py:25
  8.5 13.4 %collective-permute-start.1 = (f32[8,512]{0,1:T(8,128)S(1)}, f32[8,512]{0,1:T(8,128)S(1)}, u32[]{:S(2)}, u32[]{:S(2)}) collective-permute-start(f32[8,512]{0,1:T(8,128)S(1)} %get-tuple-element.24), channel_id=1, source_target_pairs={{4,0},{8,4},{12,8},{16,12},{20,16},{24,20},{28,24},{0,28},{5,1},{9... | collective-permute-start | bytes 49160 | tf_op jit(solution)/shard_map/ppermute | solution.py:28
  19.6 134.6 %copy-start.5 = (f32[3]{0:T(128)}, f32[3]{0:T(128)S(1)}, u32[]{:S(2)}) copy-start(f32[3]{0:T(128)S(1)} %get-tuple-element.46) | copy-start | bytes 40
  45.6 10.1 %copy-start.7 = (f32[4]{0:T(128)S(1)}, f32[4]{0:T(128)}, u32[]{:S(2)}) copy-start(f32[4]{0:T(128)} %param.16) | copy-start | bytes 52
  45.6 10.2 %copy-start.2 = (f32[2,4,2048]{2,1,0:T(4,128)S(1)}, f32[2,4,2048]{2,1,0:T(4,128)}, u32[]{:S(2)}) copy-start(f32[2,4,2048]{2,1,0:T(4,128)} %param.15) | copy-start | bytes 196612
  50.9 10.6 %collective-permute-start.2 = (f32[8,512]{0,1:T(8,128)S(1)}, f32[8,512]{0,1:T(8,128)S(1)}, u32[]{:S(2)}, u32[]{:S(2)}) collective-permute-start(f32[8,512]{0,1:T(8,128)S(1)} %get-tuple-element.21), channel_id=1, source_target_pairs={{0,4},{4,8},{8,12},{12,16},{16,20},{20,24},{24,28},{28,0},{1,5},{5... | collective-permute-start | bytes 49160 | tf_op jit(solution)/shard_map/ppermute | solution.py:25
  51.2 14.2 %collective-permute-start.3 = (f32[8,512]{0,1:T(8,128)S(1)}, f32[8,512]{0,1:T(8,128)S(1)}, u32[]{:S(2)}, u32[]{:S(2)}) collective-permute-start(f32[8,512]{0,1:T(8,128)S(1)} %get-tuple-element.22), channel_id=1, source_target_pairs={{4,0},{8,4},{12,8},{16,12},{20,16},{24,20},{28,24},{0,28},{5,1},{9... | collective-permute-start | bytes 49160 | tf_op jit(solution)/shard_map/ppermute | solution.py:28
  96.0 1.9 %copy-start = (f32[2,4,2048]{0,2,1:T(8,128)}, f32[2,4,2048]{0,2,1:T(8,128)S(1)}, u32[]{:S(2)}) copy-start(f32[2,4,2048]{0,2,1:T(8,128)S(1)} %multiply_subtract_fusion) | copy-start | bytes 196612
  97.9 56.3 %copy-start.1 = (f32[36,3,512]{2,0,1:T(8,128)S(1)}, f32[36,3,512]{2,0,1:T(8,128)}, u32[]{:S(2)}) copy-start(f32[36,3,512]{2,0,1:T(8,128)} %param.24) | copy-start | bytes 663556
  130.4 10.8 %all-to-all-start = ((f32[2,8,256]{2,0,1:T(2,128)}), f32[2,8,256]{2,0,1:T(2,128)S(1)}, u32[]{:S(2)}, u32[]{:S(2)}) async-start(f32[2,8,256]{2,0,1:T(2,128)} %multiply_bitcast_fusion), calls=%async_computation | async-start | bytes 32768 | tf_op jit(solution)/shard_map/all_to_all | solution.py:124
  155.6 8.3 %collective-permute-start.4 = (f32[108,128]{0,1:T(8,128)S(1)}, f32[108,128]{0,1:T(8,128)S(1)}, u32[]{:S(2)}, u32[]{:S(2)}) collective-permute-start(f32[108,128]{0,1:T(8,128)S(1)} %get-tuple-element.25), channel_id=1, source_target_pairs={{0,4},{4,8},{8,12},{12,16},{16,20},{20,24},{24,28},{28,0},{1,5},{5... | collective-permute-start | bytes 165896 | tf_op jit(solution)/shard_map/ppermute | solution.py:25
  156.1 7.8 %collective-permute-start.5 = (f32[108,128]{0,1:T(8,128)S(1)}, f32[108,128]{0,1:T(8,128)S(1)}, u32[]{:S(2)}, u32[]{:S(2)}) collective-permute-start(f32[108,128]{0,1:T(8,128)S(1)} %get-tuple-element.26), channel_id=1, source_target_pairs={{4,0},{8,4},{12,8},{16,12},{20,16},{24,20},{28,24},{0,28},{5,1},{9... | collective-permute-start | bytes 165896 | tf_op jit(solution)/shard_map/ppermute | solution.py:28
where the time goes:
time: 175 us; the launch traced here: 174 us
  local copies, waits for them, and re-layouts  79.9 us (46%)
  other arithmetic  31.6 us (18%)
  blocking collectives  26 us (15%)
  starting transfers between devices  19.9 us (11%)
  waiting for transfers between devices  15.6 us (9%)
    gather x2, local copies, waits for them, and re-layouts, laplace_cells(): gathered = extended[:, neighbours]  43.5 us
    psum x1, blocking collectives, local(): mean_energy, inverse = lax.psum((own_total, own_inverse), 'spec')  26 us
    ppermute x3, starting transfers between devices, padded(): lax.ppermute(lax.slice_in_dim(block, 0, width, axis=dim), axis, backward)  11.7 us
    scatter-add x1, other arithmetic, local(): jnp.zeros((2, ocean_count), jnp.float32).at[:, flat_places]  11.5 us
    unnamed x20, local copies, waits for them, and re-layouts  8.75 us
    gather x6, local copies, waits for them, and re-layouts, propagate(): upwind = extended[:, :, neighbours[border]]  7.14 us
    all_to_all x1, waiting for transfers between devices, local(): lax.all_to_all(blocks, 'cells', split_axis=1, concat_axis=1, tiled=True)  6.49 us
    ppermute x3, waiting for transfers between devices, padded(): lax.ppermute(lax.slice_in_dim(block, 0, width, axis=dim), axis, backward)  6.11 us
  transfers between devices with their start and end apart: 7, of which 4 were waited for; matrix products, arithmetic and copies ran while one was open for 8% of the time, Pallas kernels for 0%

commit v1 on v0

v1 whole, which is shorter than its diff:
```python
import functools
import math

import jax
import jax.numpy as jnp
from jax import lax
from jax.experimental import pallas as pl
from jax.experimental.pallas import tpu as pltpu
from jax.sharding import PartitionSpec as P

DIRECTIONS = 36
BANDS = 12
ROWS = 40
LANES = 128
MESH = pl.DeviceIdType.MESH

epsilon = 1e-06
wind_factor = 0.8
growth = 0.1
coupling = 4.0
dissipation = 0.05


def lane_take(tile, lane):
    return jnp.take_along_axis(tile, lane, axis=1, mode="promise_in_bounds")


def pick(tiles, lane, high, first):
    found = lane_take(tiles[0], lane)
    for j in range(1, len(tiles)):
        found = jnp.where(high == first + j, lane_take(tiles[j], lane), found)
    return found


def spread8(row):
    return jnp.broadcast_to(row, (8, row.shape[1]))


def split_index(index):
    return lax.bitwise_and(index, LANES - 1), lax.shift_right_logical(index, 7)


def kernel(
    n_cells, n_spec,
    wind, damping, atm_table, atm_coef, atm_send, send_cells, block_count, slot_weight, recv_cells,
    spectra, sea_mask, ocn_table, face_angle, face_ratio, ocn_send,
    wind_out, spectra_out,
    ext1, ext2, rim1, rim2, surf, blk_send, blk_recv, onehot, energy, means_own, means, inv_decay,
    trig, faces, ocn_rim, ocn_ext,
    atm_ssem, atm_rsem, mean_ssem, mean_rsem, surf_ssem, surf_rsem, blk_ssem, blk_rsem, ocn_ssem, ocn_rsem,
):
    me = lax.axis_index("cells")
    part = lax.axis_index("spec")
    before, after = lax.rem(me + n_cells - 1, n_cells), lax.rem(me + 1, n_cells)
    levels, cells = wind.shape[1], wind.shape[2]
    own_tiles = cells // LANES
    rim = rim1.shape[2]
    rim_tiles = rim // LANES
    bands, ocean = spectra.shape[1], spectra.shape[2]
    ocean_tiles = ocean // LANES
    slots = send_cells.shape[1]

    barrier = pltpu.get_barrier_semaphore()

    def greet_cells(step, carry):
        other = lax.rem(me + step, n_cells)
        pl.semaphore_signal(barrier, inc=1, device_id=(other, part), device_id_type=MESH)
        return carry

    def greet_spec(step, carry):
        other = lax.rem(part + step, n_spec)
        pl.semaphore_signal(barrier, inc=1, device_id=(me, other), device_id_type=MESH)
        return carry

    lax.fori_loop(1, n_cells, greet_cells, 0)
    lax.fori_loop(1, n_spec, greet_spec, 0)

    def gather_rim(ext, out):
        tiles = [ext[:, pl.ds(rim + j * LANES, LANES)] for j in range(own_tiles)]
        for t in range(2 * rim_tiles):
            lane, high = split_index(spread8(atm_send[pl.ds(t, 1), :]))
            out[t // rim_tiles, :, pl.ds((t % rim_tiles) * LANES, LANES)] = pick(tiles, lane, high, 0)

    def rim_copies(out, ext, base):
        to_before = pltpu.make_async_remote_copy(
            src_ref=out.at[0], dst_ref=ext.at[:, pl.ds(rim + cells, rim)],
            send_sem=atm_ssem.at[base], recv_sem=atm_rsem.at[base],
            device_id=(before, part), device_id_type=MESH)
        to_after = pltpu.make_async_remote_copy(
            src_ref=out.at[1], dst_ref=ext.at[:, pl.ds(0, rim)],
            send_sem=atm_ssem.at[base + 1], recv_sem=atm_rsem.at[base + 1],
            device_id=(after, part), device_id_type=MESH)
        return to_before, to_after

    def laplace(ext, store):
        def block(b, carry):
            start = pl.multiple_of(b * LANES, LANES)
            here = ext[:, pl.ds(rim + start, LANES)]
            tiles = [ext[:, pl.ds(start + j * LANES, LANES)] for j in range(2 * rim_tiles + 1)]
            total = jnp.zeros((8, LANES), jnp.float32)
            for k in range(3):
                lane, high = split_index(spread8(atm_table[pl.ds(k, 1), pl.ds(start, LANES)]))
                near = pick(tiles, lane, high - b, 0)
                total += spread8(atm_coef[pl.ds(k, 1), pl.ds(start, LANES)]) * (near - here)
            store(start, here, total)
            return carry

        lax.fori_loop(0, own_tiles, block, 0, unroll=4)

    ext1[0:levels, pl.ds(rim, cells)] = wind[0]
    ext1[levels:2 * levels, pl.ds(rim, cells)] = wind[1]
    gather_rim(ext1, rim1)
    pl.semaphore_wait(barrier, n_cells + n_spec - 2)
    first = rim_copies(rim1, ext1, 0)
    for copy in first:
        copy.start()

    mask = sea_mask[...].astype(jnp.float32)
    frequency = []
    for k in range(bands):
        value = jnp.float32(0.6 * 1.1**k)
        for s in range(1, n_spec):
            value = jnp.where(part == s, jnp.float32(0.6 * 1.1 ** (s * bands + k)), value)
        frequency.append(value)
    total = jnp.zeros((1, ocean), jnp.float32)
    inverse = jnp.zeros((1, ocean), jnp.float32)
    for k in range(bands):
        energy[k * ROWS + 32:(k + 1) * ROWS, :] = jnp.zeros((8, ocean), jnp.float32)
        band = spectra[:, k, :] * mask
        energy[k * ROWS:k * ROWS + DIRECTIONS, :] = band
        band_sum = jnp.sum(band, axis=0, keepdims=True)
        total += band_sum
        inverse += band_sum * (1.0 / jnp.full((1, ocean), frequency[k], jnp.float32))
    means_own[0:1, :] = total
    means_own[1:2, :] = inverse

    def mean_copy(other, slot):
        return pltpu.make_async_remote_copy(
            src_ref=means_own, dst_ref=means.at[slot],
            send_sem=mean_ssem.at[other], recv_sem=mean_rsem.at[slot],
            device_id=(me, other), device_id_type=MESH)

    for step in range(1, n_spec):
        mean_copy(lax.rem(part + step, n_spec), part).start()

    for copy in first:
        copy.wait_recv()

    def keep_once(start, here, lap):
        ext2[:, pl.ds(rim + start, LANES)] = lap

    laplace(ext1, keep_once)
    gather_rim(ext2, rim2)
    second = rim_copies(rim2, ext2, 2)
    for copy in second:
        copy.start()

    def mark(i, carry):
        place = lax.broadcasted_iota(jnp.int32, (ocean, slots), 0)
        hit = place == recv_cells[pl.ds(i, 1), :]
        onehot[:, pl.ds(pl.multiple_of(i * slots, LANES), slots)] = jnp.where(hit, 1.0, 0.0).astype(jnp.bfloat16)
        return carry

    lax.fori_loop(0, n_cells, mark, 0)
    heading = (lax.broadcasted_iota(jnp.int32, (ROWS, LANES), 0).astype(jnp.float32) + 0.5) * (
        2.0 * math.pi / DIRECTIONS
    )
    trig[0] = jnp.cos(heading)
    trig[1] = jnp.sin(heading)
    angle = face_angle[...]
    ratio = face_ratio[...]
    faces[0] = jnp.cos(angle) * ratio
    faces[1] = jnp.sin(angle) * ratio
    total = means_own[0:1, :]
    inverse = means_own[1:2, :]
    for step in range(1, n_spec):
        other = lax.rem(part + step, n_spec)
        mean_copy(other, other).wait_recv()
        total += means[other, 0:1, :]
        inverse += means[other, 1:2, :]
    count = DIRECTIONS * BANDS
    mean_energy = total / count
    mean_freq = mean_energy / (inverse / count + epsilon)
    squared = mean_freq * mean_freq
    for k in range(bands):
        decay = (dissipation * frequency[k]) * (mean_energy * (squared * squared))
        inv_decay[k:k + 1, :] = 1.0 / (1.0 + decay)

    for copy in second:
        copy.wait_recv()
    row = lax.broadcasted_iota(jnp.int32, (8, LANES), 0)
    rate = jnp.zeros((8, LANES), jnp.float32)
    for v in range(levels):
        rate = jnp.where(lax.rem(row, levels) == v, damping[v], rate)

    def keep_damped(start, here, lap):
        damped = ext1[:, pl.ds(rim + start, LANES)] - rate * lap
        wind_out[0, :, pl.ds(start, LANES)] = damped[0:levels]
        wind_out[1, :, pl.ds(start, LANES)] = damped[levels:2 * levels]

    laplace(ext2, keep_damped)

    def surf_copy(other):
        return pltpu.make_async_remote_copy(
            src_ref=surf, dst_ref=surf, send_sem=surf_ssem.at[other], recv_sem=surf_rsem,
            device_id=(me, other), device_id_type=MESH)

    @pl.when(part == n_spec - 1)
    def _():
        surf[0:1, :] = wind_factor * wind_out[0, levels - 1:levels, :]
        surf[1:2, :] = wind_factor * wind_out[1, levels - 1:levels, :]
        for other in range(n_spec - 1):
            surf_copy(other).start()

    @pl.when(part != n_spec - 1)
    def _():
        surf_copy(0).wait_recv()

    for g in range(n_cells // 8):
        row = lax.broadcasted_iota(jnp.int32, (8, LANES), 0)
        live = jnp.zeros((8, LANES), jnp.int32)
        for i in range(8):
            live = jnp.where(row == i, block_count[g * 8 + i], live)
        for h in range(slots // LANES):
            spot = lax.broadcasted_iota(jnp.int32, (8, LANES), 1) + h * LANES
            scale = jnp.where(spot < live, slot_weight[g * 8:g * 8 + 8, pl.ds(h * LANES, LANES)], 0.0)
            lane, high = split_index(send_cells[g * 8:g * 8 + 8, pl.ds(h * LANES, LANES)])
            for c in range(2):
                tiles = [spread8(surf[c:c + 1, pl.ds(j * LANES, LANES)]) for j in range(own_tiles)]
                blk_send[g * 8:g * 8 + 8, c, pl.ds(h * LANES, LANES)] = scale * pick(tiles, lane, high, 0)

    def block_copy(other, slot):
        return pltpu.make_async_remote_copy(
            src_ref=blk_send.at[other], dst_ref=blk_recv.at[slot],
            send_sem=blk_ssem.at[other], recv_sem=blk_rsem.at[slot],
            device_id=(other, part), device_id_type=MESH)

    def send_block(step, carry):
        block_copy(lax.rem(me + step, n_cells), me).start()
        return carry

    lax.fori_loop(1, n_cells, send_block, 0)
    blk_recv[me] = blk_send[me]

    def wait_block(step, carry):
        other = lax.rem(me + step, n_cells)
        block_copy(other, other).wait_recv()
        return carry

    lax.fori_loop(1, n_cells, wait_block, 0)

    def deposit(i, acc):
        value = blk_recv[i]
        high = value.astype(jnp.bfloat16).astype(jnp.float32)
        rest = value - high
        middle = rest.astype(jnp.bfloat16).astype(jnp.float32)
        parts = jnp.concatenate([high, middle, rest - middle, jnp.zeros_like(high)], axis=0)
        return acc + lax.dot_general(
            parts.astype(jnp.bfloat16), onehot[:, pl.ds(pl.multiple_of(i * slots, LANES), slots)],
            (((1,), (1,)), ((), ())), preferred_element_type=jnp.float32)

    acc = lax.fori_loop(0, n_cells, deposit, jnp.zeros((8, ocean), jnp.float32), unroll=8)
    wind_u = acc[0:1] + acc[2:3] + acc[4:5]
    wind_v = acc[1:2] + acc[3:4] + acc[5:6]

    for g in range(ROWS // 8):
        rows = slice(g * 8, g * 8 + 8)
        for b in range(ocean_tiles):
            at = slice(b * LANES, (b + 1) * LANES)
            along = trig[0, rows, :] * wind_u[:, at] + trig[1, rows, :] * wind_v[:, at]
            for k in range(bands):
                gain = (growth * frequency[k]) * jnp.maximum((coupling * frequency[k]) * along - 1.0, 0.0)
                spot = slice(k * ROWS + g * 8, k * ROWS + g * 8 + 8)
                ocn_ext[spot, LANES + b * LANES:LANES + (b + 1) * LANES] = (
                    energy[spot, at] * (1.0 + gain) * inv_decay[k:k + 1, at]
                )
    for side in range(2):
        lane, high = split_index(spread8(ocn_send[side:side + 1, :]))
        for r in range(bands * ROWS // 8):
            rows = slice(r * 8, r * 8 + 8)
            tiles = [ocn_ext[rows, LANES + j * LANES:LANES + (j + 1) * LANES] for j in range(ocean_tiles)]
            ocn_rim[side, rows, :] = pick(tiles, lane, high, 0)
    last = ocean + LANES
    third = (
        pltpu.make_async_remote_copy(
            src_ref=ocn_rim.at[0], dst_ref=ocn_ext.at[:, pl.ds(last, LANES)],
            send_sem=ocn_ssem.at[0], recv_sem=ocn_rsem.at[0],
            device_id=(before, part), device_id_type=MESH),
        pltpu.make_async_remote_copy(
            src_ref=ocn_rim.at[1], dst_ref=ocn_ext.at[:, pl.ds(0, LANES)],
            send_sem=ocn_ssem.at[1], recv_sem=ocn_rsem.at[1],
            device_id=(after, part), device_id_type=MESH),
    )
    for copy in third:
        copy.start()
    for copy in third:
        copy.wait_recv()

    for b in range(ocean_tiles):
        at = slice(b * LANES, (b + 1) * LANES)
        index = [split_index(spread8(ocn_table[f:f + 1, at])) for f in range(3)]
        for g in range(ROWS // 8):
            normal = [
                trig[0, g * 8:g * 8 + 8, :] * faces[0, f:f + 1, at] + trig[1, g * 8:g * 8 + 8, :] * faces[1, f:f + 1, at]
                for f in range(3)
            ]
            for k in range(bands):
                speed = 0.5 / jnp.full((8, LANES), frequency[k], jnp.float32)
                rows = slice(k * ROWS + g * 8, k * ROWS + g * 8 + 8)
                tiles = [ocn_ext[rows, (b + j) * LANES:(b + j + 1) * LANES] for j in range(3)]
                here = tiles[1]
                result = here
                for f in range(3):
                    transport = speed * normal[f]
                    upwind = pick(tiles, index[f][0], index[f][1], b)
                    result = result - transport * jnp.where(transport > 0.0, here, upwind)
                energy[rows, at] = result
    for k in range(bands):
        spectra_out[:, k, :] = energy[k * ROWS:k * ROWS + DIRECTIONS, :]

    for copy in (*first, *second, *third):
        copy.wait_send()
    for step in range(1, n_spec):
        mean_copy(lax.rem(part + step, n_spec), part).wait_send()

    @pl.when(part == n_spec - 1)
    def _():
        for other in range(n_spec - 1):
            surf_copy(other).wait_send()

    def sent_block(step, carry):
        block_copy(lax.rem(me + step, n_cells), me).wait_send()
        return carry

    lax.fori_loop(1, n_cells, sent_block, 0)


def local(
    n_cells, n_spec,
    wind_field, damping, atm_table, atm_coef, atm_send, send_cells, block_count, slot_weight, recv_cells,
    spectra, sea_mask, ocn_table, face_angle, face_ratio, ocn_send,
):
    levels, cells = wind_field.shape[1:]
    rim = atm_send.shape[0] // 2
    bands, ocean = spectra.shape[1:]
    slots = send_cells.shape[1]
    f32 = jnp.float32
    vmem = pl.BlockSpec(memory_space=pltpu.VMEM)
    smem = pl.BlockSpec(memory_space=pltpu.SMEM)
    dma = pltpu.SemaphoreType.DMA
    return pl.pallas_call(
        functools.partial(kernel, n_cells, n_spec),
        out_shape=(
            jax.ShapeDtypeStruct(wind_field.shape, f32),
            jax.ShapeDtypeStruct(spectra.shape, f32),
        ),
        in_specs=[vmem, smem, vmem, vmem, vmem, vmem, smem, vmem, vmem, vmem, vmem, vmem, vmem, vmem, vmem],
        out_specs=(vmem, vmem),
        scratch_shapes=[
            pltpu.VMEM((2 * levels, cells + 2 * rim), f32),
            pltpu.VMEM((2 * levels, cells + 2 * rim), f32),
            pltpu.VMEM((2, 2 * levels, rim), f32),
            pltpu.VMEM((2, 2 * levels, rim), f32),
            pltpu.VMEM((2, cells), f32),
            pltpu.VMEM((n_cells, 2, slots), f32),
            pltpu.VMEM((n_cells, 2, slots), f32),
            pltpu.VMEM((ocean, n_cells * slots), jnp.bfloat16),
            pltpu.VMEM((bands * ROWS, ocean), f32),
            pltpu.VMEM((2, ocean), f32),
            pltpu.VMEM((n_spec, 2, ocean), f32),
            pltpu.VMEM((bands, ocean), f32),
            pltpu.VMEM((2, ROWS, LANES), f32),
            pltpu.VMEM((2, 3, ocean), f32),
            pltpu.VMEM((2, bands * ROWS, LANES), f32),
            pltpu.VMEM((bands * ROWS, ocean + 2 * LANES), f32),
            dma((4,)), dma((4,)), dma((n_spec,)), dma((n_spec,)), dma((n_spec,)), dma,
            dma((n_cells,)), dma((n_cells,)), dma((2,)), dma((2,)),
        ],
        compiler_params=pltpu.CompilerParams(
            collective_id=0, has_side_effects=True, vmem_limit_bytes=(8 if n_cells <= 16 else 48) * 2**20
        ),
    )(
        wind_field, damping, atm_table, atm_coef, atm_send.reshape(-1, LANES), send_cells, block_count,
        slot_weight, recv_cells, spectra, sea_mask.reshape(1, -1), ocn_table, face_angle, face_ratio,
        ocn_send.reshape(-1, LANES),
    )


def solution(mesh):
    in_specs = (
        P(None, "spec", "cells"),
        P("spec"),
        P(None, "cells"),
        P(None, "cells"),
        P("cells"),
        P("cells", None),
        P("cells"),
        P("cells", None),
        P("cells", None),
        P(None, "spec", "cells"),
        P("cells"),
        P(None, "cells"),
        P(None, "cells"),
        P(None, "cells"),
        P("cells"),
    )
    out_specs = (P(None, "spec", "cells"), P(None, "spec", "cells"))
    body = functools.partial(local, mesh.shape["cells"], mesh.shape["spec"])
    return jax.shard_map(body, mesh=mesh, in_specs=in_specs, out_specs=out_specs, check_vma=False)
```

time: 175 us -> 32.3 us (0.18)
  local copies, waits for them, and re-layouts: 79.9 us -> 2.65 us
  other arithmetic: 31.6 us -> 0 us
  Pallas kernels: 0 us -> 28.6 us
  blocking collectives: 26 us -> 0 us
  starting transfers between devices: 19.9 us -> 0 us
  waiting for transfers between devices: 15.6 us -> 0 us
    gather x13 -> x0, local copies, waits for them, and re-layouts: 62.8 us -> none  [the longest x2 43.5 us: laplace_cells(): gathered = extended[:, neighbours]]
    pallas_call x0 -> x1, Pallas kernels: none -> 28.6 us  [local(): pl.pallas_call(functools.partial(kernel, n_cells, n_spec), out_shape=(jax...]
    psum x1 -> x0, blocking collectives: 26 us -> none  [local(): mean_energy, inverse = lax.psum((own_total, own_inverse), 'spec')]
    ppermute x6 -> x0, starting transfers between devices: 15.7 us -> none  [the longest x3 11.7 us: padded(): lax.ppermute(lax.slice_in_dim(block, 0, width, axis=dim), axis, backward)]
    scatter-add x1 -> x0, other arithmetic: 11.5 us -> none  [local(): jnp.zeros((2, ocean_count), jnp.float32).at[:, flat_places]]
    ppermute x6 -> x0, waiting for transfers between devices: 9.13 us -> none  [the longest x3 6.11 us: padded(): lax.ppermute(lax.slice_in_dim(block, 0, width, axis=dim), axis, backward)]
    unnamed x20 -> x30, local copies, waits for them, and re-layouts: 8.75 us -> 1.88 us
    all_to_all x1 -> x0, waiting for transfers between devices: 6.49 us -> none  [local(): lax.all_to_all(blocks, 'cells', split_axis=1, concat_axis=1, tiled=True)]
  transfers between devices with their start and end apart: 7 -> 0, of which waited for: 4 -> 0; matrix products, arithmetic and copies ran while one was open for 8% -> 0% of each run, Pallas kernels for 0% -> 0%
where the time goes in v1:
time: 32.3 us; the launch traced here: 32.1 us
  Pallas kernels  28.6 us (89%)
  local copies, waits for them, and re-layouts  2.65 us (8%)
  between operations  0.87 us (3%)
    pallas_call x1, Pallas kernels, local(): pl.pallas_call(functools.partial(kernel, n_cells, n_spec), out_shape=(jax...  28.6 us
    unnamed x30, local copies, waits for them, and re-layouts  1.88 us
    pallas_call x1, local copies, waits for them, and re-layouts, local(): pl.pallas_call(functools.partial(kernel, n_cells, n_spec), out_shape=(jax...  0.76 us

profile of v1, /device:TPU:0, one launch (start us, length us, event | category | flops | bytes accessed | tf_op | source)
XLA Modules:
  0.0 32.1 jit_solution(6626204570242022328)
XLA Ops:
  0.6 0.0 copy-start
  0.6 0.0 copy-start.1
  0.7 0.0 copy-start.2
  0.7 0.0 copy-start.3
  0.7 0.0 copy-start.4
  0.7 0.0 copy-start.5
  0.7 0.0 copy-start.6
  0.7 0.0 copy-start.7
  0.7 0.0 copy-start.8
  0.7 0.0 copy-start.9
  0.7 0.0 copy-start.10
  0.7 0.0 copy-start.11
  0.8 0.0 copy-start.12
  0.8 0.0 copy-start.13
  0.8 1.2 %copy.17.spectra = f32[36,3,512]{2,1,0:T(4,128)S(1)} copy(f32[36,3,512]{2,0,1:T(8,128)} %param.24) | data formatting | bytes 442368 | tf_op args[9]
  2.0 0.0 copy-done
  2.0 0.0 copy-done.1
  2.0 0.0 copy-done.2
  2.0 0.0 copy-done.3
  2.0 0.0 copy-done.4
  2.0 0.0 copy-done.5
  2.0 0.0 copy-done.6
  2.0 0.0 copy-done.7
  2.1 0.0 copy-done.8
  2.1 0.0 copy-done.9
  2.1 0.0 copy-done.10
  2.1 0.0 copy-done.11
  2.1 0.0 copy-done.12
  2.1 0.0 copy-done.13
  2.1 28.6 %shard_map.158 = (f32[2,4,2048]{2,1,0:T(4,128)S(1)}, f32[36,3,512]{2,1,0:T(4,128)S(1)}) custom-call(f32[2,4,2048]{2,1,0:T(4,128)S(1)} %copy-done, f32[4]{0:T(128)S(1)} %copy-done.12, s32[3,2048]{1,0:T(4,128)S(1)} %copy-done.1, f32[3,2048]{1,0:T(4,128)S(1)} %copy-done.2, s32[8,128]{1,0:T(8,128)S(1)} %bitcast.3, s32[8,256]{1,0:T(8,128)S(1)} %copy-done.3, ...), custom_call_target="tpu_custom_call" | custom-call | tf_op jit(solution)/shard_map/pallas_call | solution.py:351
  30.7 0.8 %copy.18 = f32[36,3,512]{2,0,1:T(8,128)} copy(f32[36,3,512]{2,1,0:T(4,128)S(1)} %get-tuple-element.3) | data formatting | bytes 442368 | tf_op jit(solution)/shard_map/pallas_call | solution.py:351
  31.5 0.6 %copy.20 = f32[2,4,2048]{2,1,0:T(4,128)} copy(f32[2,4,2048]{2,1,0:T(4,128)S(1)} %get-tuple-element.6) | data formatting | bytes 131072
Async XLA Ops:
  0.6 1.3 %copy-start = (f32[2,4,2048]{2,1,0:T(4,128)S(1)}, f32[2,4,2048]{2,1,0:T(4,128)}, u32[]{:S(2)}) copy-start(f32[2,4,2048]{2,1,0:T(4,128)} %wind.1) | copy-start | bytes 196612
  0.6 1.3 %copy-start.1 = (s32[3,2048]{1,0:T(4,128)S(1)}, s32[3,2048]{1,0:T(4,128)}, u32[]{:S(2)}) copy-start(s32[3,2048]{1,0:T(4,128)} %atm_table.1) | copy-start | bytes 73732
  0.7 1.3 %copy-start.2 = (f32[3,2048]{1,0:T(4,128)S(1)}, f32[3,2048]{1,0:T(4,128)}, u32[]{:S(2)}) copy-start(f32[3,2048]{1,0:T(4,128)} %atm_coef.1) | copy-start | bytes 73732
  0.7 1.3 %copy-start.3 = (s32[8,256]{1,0:T(8,128)S(1)}, s32[8,256]{1,0:T(8,128)}, u32[]{:S(2)}) copy-start(s32[8,256]{1,0:T(8,128)} %send_cells.1) | copy-start | bytes 24580
  0.7 1.3 %copy-start.4 = (f32[8,256]{1,0:T(8,128)S(1)}, f32[8,256]{1,0:T(8,128)}, u32[]{:S(2)}) copy-start(f32[8,256]{1,0:T(8,128)} %slot_weight.1) | copy-start | bytes 24580
  0.7 1.3 %copy-start.5 = (s32[8,256]{1,0:T(8,128)S(1)}, s32[8,256]{1,0:T(8,128)}, u32[]{:S(2)}) copy-start(s32[8,256]{1,0:T(8,128)} %recv_cells.1) | copy-start | bytes 24580
  0.7 1.3 %copy-start.6 = (s32[3,512]{1,0:T(4,128)S(1)}, s32[3,512]{1,0:T(4,128)}, u32[]{:S(2)}) copy-start(s32[3,512]{1,0:T(4,128)} %ocn_table.1) | copy-start | bytes 18436
  0.7 1.3 %copy-start.7 = (f32[3,512]{1,0:T(4,128)S(1)}, f32[3,512]{1,0:T(4,128)}, u32[]{:S(2)}) copy-start(f32[3,512]{1,0:T(4,128)} %face_angle.1) | copy-start | bytes 18436
  0.7 1.3 %copy-start.8 = (f32[3,512]{1,0:T(4,128)S(1)}, f32[3,512]{1,0:T(4,128)}, u32[]{:S(2)}) copy-start(f32[3,512]{1,0:T(4,128)} %face_ratio.1) | copy-start | bytes 18436
  0.7 1.3 %copy-start.9 = (s32[1024]{0:T(1024)S(1)}, s32[1024]{0:T(1024)}, u32[]{:S(2)}) copy-start(s32[1024]{0:T(1024)} %param.19) | copy-start | bytes 12292
  0.7 1.3 %copy-start.10 = (s32[512]{0:T(512)S(1)}, s32[512]{0:T(512)}, u32[]{:S(2)}) copy-start(s32[512]{0:T(512)} %param.25) | copy-start | bytes 6148
  0.7 1.3 %copy-start.11 = (s32[256]{0:T(256)S(1)}, s32[256]{0:T(256)}, u32[]{:S(2)}) copy-start(s32[256]{0:T(256)} %param.29) | copy-start | bytes 3076
  0.8 1.3 %copy-start.12 = (f32[4]{0:T(128)S(1)}, f32[4]{0:T(128)}, u32[]{:S(2)}) copy-start(f32[4]{0:T(128)} %damping.1) | copy-start | bytes 52
  0.8 1.3 %copy-start.13 = (s32[8]{0:T(128)S(1)}, s32[8]{0:T(128)}, u32[]{:S(2)}) copy-start(s32[8]{0:T(128)} %block_count.1) | copy-start | bytes 100

commit v2 on v1

--- a/solution.py
+++ b/solution.py
@@ -13,6 +13,10 @@
 ROWS = 40
 LANES = 128
 MESH = pl.DeviceIdType.MESH
+LOADED = (
+    "wind", "atm_send", "spectra", "sea_mask", "atm_table", "atm_coef", "recv_cells", "ocn_send", "face_angle",
+    "face_ratio", "slot_weight", "send_cells", "ocn_table",
+)
 
 epsilon = 1e-06
 wind_factor = 0.8
@@ -42,13 +46,16 @@
 
 def kernel(
     n_cells, n_spec,
-    wind, damping, atm_table, atm_coef, atm_send, send_cells, block_count, slot_weight, recv_cells,
-    spectra, sea_mask, ocn_table, face_angle, face_ratio, ocn_send,
-    wind_out, spectra_out,
-    ext1, ext2, rim1, rim2, surf, blk_send, blk_recv, onehot, energy, means_own, means, inv_decay,
-    trig, faces, ocn_rim, ocn_ext,
-    atm_ssem, atm_rsem, mean_ssem, mean_rsem, surf_ssem, surf_rsem, blk_ssem, blk_rsem, ocn_ssem, ocn_rsem,
+    damping, block_count, *refs,
 ):
+    count = len(LOADED)
+    given, (wind_out, spectra_out), held = refs[:count], refs[count:count + 2], refs[count + 2:2 * count + 2]
+    (wind, atm_send, spectra, sea_mask, atm_table, atm_coef, recv_cells, ocn_send, face_angle, face_ratio, slot_weight,
+     send_cells, ocn_table) = held
+    (ext1, ext2, rim1, rim2, surf, blk_send, blk_recv, onehot, onehot_rim, near_recv, near_send, means_own, means,
+     trig, faces, ocn_rim, ocn_ext,
+     load_sem, atm_ssem, atm_rsem, mean_ssem, mean_rsem, surf_ssem, surf_rsem, blk_ssem, blk_rsem, ocn_ssem, ocn_rsem,
+     near_ssem, near_rsem) = refs[2 * count + 2:]
     me = lax.axis_index("cells")
     part = lax.axis_index("spec")
     before, after = lax.rem(me + n_cells - 1, n_cells), lax.rem(me + 1, n_cells)
@@ -56,9 +63,10 @@
     own_tiles = cells // LANES
     rim = rim1.shape[2]
     rim_tiles = rim // LANES
-    bands, ocean = spectra.shape[1], spectra.shape[2]
+    bands, ocean = spectra.shape[0], spectra.shape[2]
     ocean_tiles = ocean // LANES
     slots = send_cells.shape[1]
+    stored = n_cells <= 16
 
     barrier = pltpu.get_barrier_semaphore()
 
@@ -74,6 +82,10 @@
 
     lax.fori_loop(1, n_cells, greet_cells, 0)
     lax.fori_loop(1, n_spec, greet_spec, 0)
+
+    loads = [pltpu.make_async_copy(given[q], held[q], load_sem.at[q]) for q in range(count)]
+    for load in loads:
+        load.start()
 
     def gather_rim(ext, out):
         tiles = [ext[:, pl.ds(rim + j * LANES, LANES)] for j in range(own_tiles)]
@@ -107,12 +119,30 @@
 
         lax.fori_loop(0, own_tiles, block, 0, unroll=4)
 
+    for load in loads[:2]:
+        load.wait()
     ext1[0:levels, pl.ds(rim, cells)] = wind[0]
     ext1[levels:2 * levels, pl.ds(rim, cells)] = wind[1]
     gather_rim(ext1, rim1)
     pl.semaphore_wait(barrier, n_cells + n_spec - 2)
     first = rim_copies(rim1, ext1, 0)
     for copy in first:
+        copy.start()
+
+    for load in loads[2:]:
+        load.wait()
+
+    def near_copies(side, other):
+        at = 1 - side
+        return [
+            pltpu.make_async_remote_copy(
+                src_ref=src, dst_ref=dst.at[at], send_sem=near_ssem.at[2 * at + q], recv_sem=near_rsem.at[2 * at + q],
+                device_id=(other, part), device_id_type=MESH)
+            for q, (src, dst) in enumerate(((recv_cells, near_recv), (ocn_send, near_send)))
+        ]
+
+    near = near_copies(0, before) + near_copies(1, after)
+    for copy in near:
         copy.start()
 
     mask = sea_mask[...].astype(jnp.float32)
@@ -125,10 +155,7 @@
     total = jnp.zeros((1, ocean), jnp.float32)
     inverse = jnp.zeros((1, ocean), jnp.float32)
     for k in range(bands):
-        energy[k * ROWS + 32:(k + 1) * ROWS, :] = jnp.zeros((8, ocean), jnp.float32)
-        band = spectra[:, k, :] * mask
-        energy[k * ROWS:k * ROWS + DIRECTIONS, :] = band
-        band_sum = jnp.sum(band, axis=0, keepdims=True)
+        band_sum = jnp.sum(spectra[k] * mask, axis=0, keepdims=True)
         total += band_sum
         inverse += band_sum * (1.0 / jnp.full((1, ocean), frequency[k], jnp.float32))
     means_own[0:1, :] = total
@@ -155,13 +182,26 @@
     for copy in second:
         copy.start()
 
-    def mark(i, carry):
+    def hits(i):
         place = lax.broadcasted_iota(jnp.int32, (ocean, slots), 0)
-        hit = place == recv_cells[pl.ds(i, 1), :]
-        onehot[:, pl.ds(pl.multiple_of(i * slots, LANES), slots)] = jnp.where(hit, 1.0, 0.0).astype(jnp.bfloat16)
-        return carry
-
-    lax.fori_loop(0, n_cells, mark, 0)
+        return jnp.where(place == recv_cells[pl.ds(i, 1), :], 1.0, 0.0).astype(jnp.bfloat16)
+
+    def rim_hits(side, column, i):
+        return jnp.where(column == near_recv[side, pl.ds(i, 1), :], 1.0, 0.0).astype(jnp.bfloat16)
+
+    for copy in near:
+        copy.wait_recv()
+    columns = []
+    for side in range(2):
+        names = near_send[side, 1 - side:2 - side, :].astype(jnp.float32)
+        column = jnp.transpose(jnp.broadcast_to(names, (LANES, LANES))).astype(jnp.int32)
+        columns.append(jnp.concatenate([column] * (slots // LANES), axis=1))
+    if stored:
+        for i in range(n_cells):
+            at = slice(i * slots, (i + 1) * slots)
+            onehot[:, at] = hits(i)
+            for side in range(2):
+                onehot_rim[side, :, at] = rim_hits(side, columns[side], i)
     heading = (lax.broadcasted_iota(jnp.int32, (ROWS, LANES), 0).astype(jnp.float32) + 0.5) * (
         2.0 * math.pi / DIRECTIONS
     )
@@ -178,13 +218,33 @@
         mean_copy(other, other).wait_recv()
         total += means[other, 0:1, :]
         inverse += means[other, 1:2, :]
-    count = DIRECTIONS * BANDS
-    mean_energy = total / count
-    mean_freq = mean_energy / (inverse / count + epsilon)
+    components = DIRECTIONS * BANDS
+    mean_energy = total / components
+    mean_freq = mean_energy / (inverse / components + epsilon)
     squared = mean_freq * mean_freq
     for k in range(bands):
         decay = (dissipation * frequency[k]) * (mean_energy * (squared * squared))
-        inv_decay[k:k + 1, :] = 1.0 / (1.0 + decay)
+        own = pl.ds(LANES, ocean)
+        ocn_ext[k * ROWS + 32:(k + 1) * ROWS, own] = jnp.zeros((8, ocean), jnp.float32)
+        ocn_ext[k * ROWS:k * ROWS + DIRECTIONS, own] = spectra[k] * (mask * (1.0 / (1.0 + decay)))
+    for side in range(2):
+        lane, high = split_index(spread8(ocn_send[side:side + 1, :]))
+        for r in range(bands * ROWS // 8):
+            rows = slice(r * 8, r * 8 + 8)
+            tiles = [ocn_ext[rows, LANES + j * LANES:LANES + (j + 1) * LANES] for j in range(ocean_tiles)]
+            ocn_rim[side, rows, :] = pick(tiles, lane, high, 0)
+    third = (
+        pltpu.make_async_remote_copy(
+            src_ref=ocn_rim.at[0], dst_ref=ocn_ext.at[:, pl.ds(ocean + LANES, LANES)],
+            send_sem=ocn_ssem.at[0], recv_sem=ocn_rsem.at[0],
+            device_id=(before, part), device_id_type=MESH),
+        pltpu.make_async_remote_copy(
+            src_ref=ocn_rim.at[1], dst_ref=ocn_ext.at[:, pl.ds(0, LANES)],
+            send_sem=ocn_ssem.at[1], recv_sem=ocn_rsem.at[1],
+            device_id=(after, part), device_id_type=MESH),
+    )
+    for copy in third:
+        copy.start()
 
     for copy in second:
         copy.wait_recv()
@@ -227,11 +287,14 @@
             lane, high = split_index(send_cells[g * 8:g * 8 + 8, pl.ds(h * LANES, LANES)])
             for c in range(2):
                 tiles = [spread8(surf[c:c + 1, pl.ds(j * LANES, LANES)]) for j in range(own_tiles)]
-                blk_send[g * 8:g * 8 + 8, c, pl.ds(h * LANES, LANES)] = scale * pick(tiles, lane, high, 0)
+                blk_send[g * 8 + 1:g * 8 + 9, c, pl.ds(h * LANES, LANES)] = scale * pick(tiles, lane, high, 0)
+
+    blk_send[0] = blk_send[n_cells]
+    blk_send[n_cells + 1] = blk_send[1]
 
     def block_copy(other, slot):
         return pltpu.make_async_remote_copy(
-            src_ref=blk_send.at[other], dst_ref=blk_recv.at[slot],
+            src_ref=blk_send.at[pl.ds(other, 3)], dst_ref=blk_recv.at[slot],
             send_sem=blk_ssem.at[other], recv_sem=blk_rsem.at[slot],
             device_id=(other, part), device_id_type=MESH)
 
@@ -240,7 +303,8 @@
         return carry
 
     lax.fori_loop(1, n_cells, send_block, 0)
-    blk_recv[me] = blk_send[me]
+    for r in range(3):
+        blk_recv[me, r] = blk_send[me + r]
 
     def wait_block(step, carry):
         other = lax.rem(me + step, n_cells)
@@ -249,52 +313,43 @@
 
     lax.fori_loop(1, n_cells, wait_block, 0)
 
-    def deposit(i, acc):
-        value = blk_recv[i]
+    def product(value, ones):
         high = value.astype(jnp.bfloat16).astype(jnp.float32)
         rest = value - high
         middle = rest.astype(jnp.bfloat16).astype(jnp.float32)
         parts = jnp.concatenate([high, middle, rest - middle, jnp.zeros_like(high)], axis=0)
-        return acc + lax.dot_general(
-            parts.astype(jnp.bfloat16), onehot[:, pl.ds(pl.multiple_of(i * slots, LANES), slots)],
-            (((1,), (1,)), ((), ())), preferred_element_type=jnp.float32)
-
-    acc = lax.fori_loop(0, n_cells, deposit, jnp.zeros((8, ocean), jnp.float32), unroll=8)
+        return lax.dot_general(
+            parts.astype(jnp.bfloat16), ones, (((1,), (1,)), ((), ())), preferred_element_type=jnp.float32)
+
+    def deposit(i, sums):
+        if stored:
+            at = slice(i * slots, (i + 1) * slots)
+            ones = [onehot_rim[0, :, at], onehot[:, at], onehot_rim[1, :, at]]
+        else:
+            ones = [rim_hits(0, columns[0], i), hits(i), rim_hits(1, columns[1], i)]
+        return tuple(acc + product(blk_recv[i, r], ones[r]) for r, acc in enumerate(sums))
+
+    sums = tuple(jnp.zeros((8, width), jnp.float32) for width in (LANES, ocean, LANES))
+    if stored:
+        for i in range(n_cells):
+            sums = deposit(i, sums)
+    else:
+        sums = lax.fori_loop(0, n_cells, deposit, sums)
+    acc = jnp.concatenate(sums, axis=1)
     wind_u = acc[0:1] + acc[2:3] + acc[4:5]
     wind_v = acc[1:2] + acc[3:4] + acc[5:6]
 
+    for copy in third:
+        copy.wait_recv()
     for g in range(ROWS // 8):
         rows = slice(g * 8, g * 8 + 8)
-        for b in range(ocean_tiles):
+        for b in range(ocean_tiles + 2):
             at = slice(b * LANES, (b + 1) * LANES)
             along = trig[0, rows, :] * wind_u[:, at] + trig[1, rows, :] * wind_v[:, at]
             for k in range(bands):
                 gain = (growth * frequency[k]) * jnp.maximum((coupling * frequency[k]) * along - 1.0, 0.0)
                 spot = slice(k * ROWS + g * 8, k * ROWS + g * 8 + 8)
-                ocn_ext[spot, LANES + b * LANES:LANES + (b + 1) * LANES] = (
-                    energy[spot, at] * (1.0 + gain) * inv_decay[k:k + 1, at]
-                )
-    for side in range(2):
-        lane, high = split_index(spread8(ocn_send[side:side + 1, :]))
-        for r in range(bands * ROWS // 8):
-            rows = slice(r * 8, r * 8 + 8)
-            tiles = [ocn_ext[rows, LANES + j * LANES:LANES + (j + 1) * LANES] for j in range(ocean_tiles)]
-            ocn_rim[side, rows, :] = pick(tiles, lane, high, 0)
-    last = ocean + LANES
-    third = (
-        pltpu.make_async_remote_copy(
-            src_ref=ocn_rim.at[0], dst_ref=ocn_ext.at[:, pl.ds(last, LANES)],
-            send_sem=ocn_ssem.at[0], recv_sem=ocn_rsem.at[0],
-            device_id=(before, part), device_id_type=MESH),
-        pltpu.make_async_remote_copy(
-            src_ref=ocn_rim.at[1], dst_ref=ocn_ext.at[:, pl.ds(0, LANES)],
-            send_sem=ocn_ssem.at[1], recv_sem=ocn_rsem.at[1],
-            device_id=(after, part), device_id_type=MESH),
-    )
-    for copy in third:
-        copy.start()
-    for copy in third:
-        copy.wait_recv()
+                ocn_ext[spot, at] = ocn_ext[spot, at] * (1.0 + gain)
 
     for b in range(ocean_tiles):
         at = slice(b * LANES, (b + 1) * LANES)
@@ -314,11 +369,9 @@
                     transport = speed * normal[f]
                     upwind = pick(tiles, index[f][0], index[f][1], b)
                     result = result - transport * jnp.where(transport > 0.0, here, upwind)
-                energy[rows, at] = result
-    for k in range(bands):
-        spectra_out[:, k, :] = energy[k * ROWS:k * ROWS + DIRECTIONS, :]
-
-    for copy in (*first, *second, *third):
+                size = min(8, DIRECTIONS - g * 8)
+                spectra_out[k, g * 8:g * 8 + size, at] = result[0:size]
+    for copy in (*first, *second, *third, *near):
         copy.wait_send()
     for step in range(1, n_spec):
         mean_copy(lax.rem(part + step, n_spec), part).wait_send()
@@ -347,43 +400,51 @@
     f32 = jnp.float32
     vmem = pl.BlockSpec(memory_space=pltpu.VMEM)
     smem = pl.BlockSpec(memory_space=pltpu.SMEM)
+    hbm = pl.BlockSpec(memory_space=pltpu.HBM)
     dma = pltpu.SemaphoreType.DMA
-    return pl.pallas_call(
+    loaded = dict(
+        wind=wind_field, atm_send=atm_send.reshape(-1, LANES), spectra=jnp.transpose(spectra, (1, 0, 2)),
+        sea_mask=sea_mask.reshape(1, -1), atm_table=atm_table, atm_coef=atm_coef, recv_cells=recv_cells,
+        ocn_send=ocn_send.reshape(-1, LANES), face_angle=face_angle, face_ratio=face_ratio, slot_weight=slot_weight,
+        send_cells=send_cells, ocn_table=ocn_table,
+    )
+    loaded = [loaded[name] for name in LOADED]
+    held_slots = n_cells * slots if n_cells <= 16 else LANES
+    wind_out, spectra_out = pl.pallas_call(
         functools.partial(kernel, n_cells, n_spec),
         out_shape=(
             jax.ShapeDtypeStruct(wind_field.shape, f32),
-            jax.ShapeDtypeStruct(spectra.shape, f32),
+            jax.ShapeDtypeStruct((bands, DIRECTIONS, ocean), f32),
         ),
-        in_specs=[vmem, smem, vmem, vmem, vmem, vmem, smem, vmem, vmem, vmem, vmem, vmem, vmem, vmem, vmem],
+        in_specs=[smem, smem] + [hbm] * len(loaded),
         out_specs=(vmem, vmem),
         scratch_shapes=[
+            *(pltpu.VMEM(array.shape, array.dtype) for array in loaded),
             pltpu.VMEM((2 * levels, cells + 2 * rim), f32),
             pltpu.VMEM((2 * levels, cells + 2 * rim), f32),
             pltpu.VMEM((2, 2 * levels, rim), f32),
             pltpu.VMEM((2, 2 * levels, rim), f32),
             pltpu.VMEM((2, cells), f32),
-            pltpu.VMEM((n_cells, 2, slots), f32),
-            pltpu.VMEM((n_cells, 2, slots), f32),
-            pltpu.VMEM((ocean, n_cells * slots), jnp.bfloat16),
-            pltpu.VMEM((bands * ROWS, ocean), f32),
+            pltpu.VMEM((n_cells + 2, 2, slots), f32),
+            pltpu.VMEM((n_cells, 3, 2, slots), f32),
+            pltpu.VMEM((ocean, held_slots), jnp.bfloat16),
+            pltpu.VMEM((2, LANES, held_slots), jnp.bfloat16),
+            pltpu.VMEM((2, n_cells, slots), jnp.int32),
+            pltpu.VMEM((2, 2, LANES), jnp.int32),
             pltpu.VMEM((2, ocean), f32),
             pltpu.VMEM((n_spec, 2, ocean), f32),
-            pltpu.VMEM((bands, ocean), f32),
             pltpu.VMEM((2, ROWS, LANES), f32),
             pltpu.VMEM((2, 3, ocean), f32),
             pltpu.VMEM((2, bands * ROWS, LANES), f32),
             pltpu.VMEM((bands * ROWS, ocean + 2 * LANES), f32),
-            dma((4,)), dma((4,)), dma((n_spec,)), dma((n_spec,)), dma((n_spec,)), dma,
-            dma((n_cells,)), dma((n_cells,)), dma((2,)), dma((2,)),
+            dma((len(loaded),)), dma((4,)), dma((4,)), dma((n_spec,)), dma((n_spec,)), dma((n_spec,)), dma,
+            dma((n_cells,)), dma((n_cells,)), dma((2,)), dma((2,)), dma((4,)), dma((4,)),
         ],
         compiler_params=pltpu.CompilerParams(
-            collective_id=0, has_side_effects=True, vmem_limit_bytes=(8 if n_cells <= 16 else 48) * 2**20
+            collective_id=0, has_side_effects=True, vmem_limit_bytes=60 * 2**20
         ),
-    )(
-        wind_field, damping, atm_table, atm_coef, atm_send.reshape(-1, LANES), send_cells, block_count,
-        slot_weight, recv_cells, spectra, sea_mask.reshape(1, -1), ocn_table, face_angle, face_ratio,
-        ocn_send.reshape(-1, LANES),
-    )
+    )(damping, block_count, *loaded)
+    return wind_out, jnp.transpose(spectra_out, (1, 0, 2))
 
 
 def solution(mesh):

time: 32.3 us -> 28.2 us (0.87)
  Pallas kernels: 28.6 us -> 24.2 us
  local copies, waits for them, and re-layouts: 2.65 us -> 3.13 us
    pallas_call x1, Pallas kernels: 28.6 us -> 24.2 us  [local(): pl.pallas_call(functools.partial(kernel, n_cells, n_spec), out_shape=(jax...]
    unnamed x30 -> x2, local copies, waits for them, and re-layouts: 1.88 us -> 3.13 us
    pallas_call x1 -> x0, local copies, waits for them, and re-layouts: 0.76 us -> none  [local(): pl.pallas_call(functools.partial(kernel, n_cells, n_spec), out_shape=(jax...]
where the time goes in v2:
time: 28.2 us; the launch traced here: 28 us
  Pallas kernels  24.2 us (86%)
  local copies, waits for them, and re-layouts  3.13 us (11%)
  between operations  0.64 us (2%)
    pallas_call x1, Pallas kernels, local(): pl.pallas_call(functools.partial(kernel, n_cells, n_spec), out_shape=(jax...  24.2 us
    unnamed x2, local copies, waits for them, and re-layouts  3.13 us

profile of v2, /device:TPU:0, one launch (start us, length us, event | category | flops | bytes accessed | tf_op | source)
XLA Modules:
  0.0 28.0 jit_solution(10967628310319056257)
XLA Ops:
  0.6 24.2 %shard_map.158 = (f32[2,4,2048]{2,1,0:T(4,128)}, f32[3,36,512]{2,1,0:T(8,128)}) custom-call(f32[4]{0:T(128)} %damping.1, s32[8]{0:T(128)} %block_count.1, f32[2,4,2048]{2,1,0:T(4,128)} %refs_0_.1, s32[8,128]{1,0:T(8,128)} %bitcast.7, f32[3,36,512]{2,1,0:T(8,128)} %bitcast.5, s32[1,512]{1,0:T(1,128)} %bitcast.8, s32[3,2048]{1,0:T(4,128)} %refs_4_.1, ...), custom_call_target="tpu_custom_call" | custom-call | tf_op jit(solution)/shard_map/pallas_call | solution.py:413
  24.8 1.5 %copy.19 = f32[2,4,2048]{2,1,0:T(4,128)} copy(f32[2,4,2048]{2,1,0:T(4,128)} %get-tuple-element.8) | data formatting | bytes 131072
  26.3 1.7 %copy.20 = f32[36,3,512]{2,0,1:T(8,128)} copy(f32[36,3,512]{2,0,1:T(8,128)} %bitcast.6) | data formatting | bytes 442368

commit v3 on v2

--- a/solution.py
+++ b/solution.py
@@ -15,7 +15,7 @@
 MESH = pl.DeviceIdType.MESH
 LOADED = (
     "wind", "atm_send", "spectra", "sea_mask", "atm_table", "atm_coef", "recv_cells", "ocn_send", "face_angle",
-    "face_ratio", "slot_weight", "send_cells", "ocn_table",
+    "face_ratio", "slot_weight", "send_cells", "ocn_table", "damping", "block_count",
 )
 
 epsilon = 1e-06
@@ -46,12 +46,12 @@
 
 def kernel(
     n_cells, n_spec,
-    damping, block_count, *refs,
+    *refs,
 ):
     count = len(LOADED)
     given, (wind_out, spectra_out), held = refs[:count], refs[count:count + 2], refs[count + 2:2 * count + 2]
     (wind, atm_send, spectra, sea_mask, atm_table, atm_coef, recv_cells, ocn_send, face_angle, face_ratio, slot_weight,
-     send_cells, ocn_table) = held
+     send_cells, ocn_table, damping, block_count) = held
     (ext1, ext2, rim1, rim2, surf, blk_send, blk_recv, onehot, onehot_rim, near_recv, near_send, means_own, means,
      trig, faces, ocn_rim, ocn_ext,
      load_sem, atm_ssem, atm_rsem, mean_ssem, mean_rsem, surf_ssem, surf_rsem, blk_ssem, blk_rsem, ocn_ssem, ocn_rsem,
@@ -399,16 +399,15 @@
     slots = send_cells.shape[1]
     f32 = jnp.float32
     vmem = pl.BlockSpec(memory_space=pltpu.VMEM)
-    smem = pl.BlockSpec(memory_space=pltpu.SMEM)
     hbm = pl.BlockSpec(memory_space=pltpu.HBM)
     dma = pltpu.SemaphoreType.DMA
     loaded = dict(
         wind=wind_field, atm_send=atm_send.reshape(-1, LANES), spectra=jnp.transpose(spectra, (1, 0, 2)),
         sea_mask=sea_mask.reshape(1, -1), atm_table=atm_table, atm_coef=atm_coef, recv_cells=recv_cells,
         ocn_send=ocn_send.reshape(-1, LANES), face_angle=face_angle, face_ratio=face_ratio, slot_weight=slot_weight,
-        send_cells=send_cells, ocn_table=ocn_table,
+        send_cells=send_cells, ocn_table=ocn_table, damping=damping, block_count=block_count,
     )
-    loaded = [loaded[name] for name in LOADED]
+    loaded = [pltpu.with_memory_space_constraint(loaded[name], pltpu.HBM) for name in LOADED]
     held_slots = n_cells * slots if n_cells <= 16 else LANES
     wind_out, spectra_out = pl.pallas_call(
         functools.partial(kernel, n_cells, n_spec),
@@ -416,10 +415,11 @@
             jax.ShapeDtypeStruct(wind_field.shape, f32),
             jax.ShapeDtypeStruct((bands, DIRECTIONS, ocean), f32),
         ),
-        in_specs=[smem, smem] + [hbm] * len(loaded),
+        in_specs=[hbm] * len(loaded),
         out_specs=(vmem, vmem),
         scratch_shapes=[
-            *(pltpu.VMEM(array.shape, array.dtype) for array in loaded),
+            *(pltpu.VMEM(array.shape, array.dtype) for array in loaded[:-2]),
+            *(pltpu.SMEM(array.shape, array.dtype) for array in loaded[-2:]),
             pltpu.VMEM((2 * levels, cells + 2 * rim), f32),
             pltpu.VMEM((2 * levels, cells + 2 * rim), f32),
             pltpu.VMEM((2, 2 * levels, rim), f32),
@@ -441,9 +441,9 @@
             dma((n_cells,)), dma((n_cells,)), dma((2,)), dma((2,)), dma((4,)), dma((4,)),
         ],
         compiler_params=pltpu.CompilerParams(
-            collective_id=0, has_side_effects=True, vmem_limit_bytes=60 * 2**20
+            collective_id=0, has_side_effects=True, vmem_limit_bytes=32 * 2**20
         ),
-    )(damping, block_count, *loaded)
+    )(*loaded)
     return wind_out, jnp.transpose(spectra_out, (1, 0, 2))
 
 

time: 28.2 us -> 25 us (0.89)
  local copies, waits for them, and re-layouts: 3.13 us -> 1.32 us
  Pallas kernels: 24.2 us -> 22.8 us
    unnamed x2, local copies, waits for them, and re-layouts: 3.13 us -> 1.32 us
    pallas_call x1, Pallas kernels: 24.2 us -> 22.8 us  [local(): pl.pallas_call(functools.partial(kernel, n_cells, n_spec), out_shape=(jax...]
where the time goes in v3:
time: 25 us; the launch traced here: 24.8 us
  Pallas kernels  22.8 us (91%)
  local copies, waits for them, and re-layouts  1.32 us (5%)
  between operations  0.64 us (3%)
    pallas_call x1, Pallas kernels, local(): pl.pallas_call(functools.partial(kernel, n_cells, n_spec), out_shape=(jax...  22.8 us
    unnamed x2, local copies, waits for them, and re-layouts  1.32 us

profile of v3, /device:TPU:0, one launch (start us, length us, event | category | flops | bytes accessed | tf_op | source)
XLA Modules:
  0.0 24.8 jit_solution(1970976610667560587)
XLA Ops:
  0.6 22.8 %shard_map.158 = (f32[2,4,2048]{2,1,0:T(4,128)S(1)}, f32[3,36,512]{2,1,0:T(8,128)S(1)}) custom-call(f32[2,4,2048]{2,1,0:T(4,128)} %refs_0_.1, s32[8,128]{1,0:T(8,128)} %bitcast.7, f32[3,36,512]{2,1,0:T(8,128)} %bitcast.6, s32[1,512]{1,0:T(1,128)} %bitcast.8, s32[3,2048]{1,0:T(4,128)} %refs_4_.1, f32[3,2048]{1,0:T(4,128)} %refs_5_.1, s32[8,256]{1,0:T(8,128)} %refs_6_.1, ...), custom_call_target="tpu_custom_call" | custom-call | tf_op jit(solution)/shard_map/pallas_call | solution.py:412
  23.5 0.6 %copy.19 = f32[2,4,2048]{2,1,0:T(4,128)} copy(f32[2,4,2048]{2,1,0:T(4,128)S(1)} %get-tuple-element.8) | data formatting | bytes 131072
  24.1 0.7 %copy.20 = f32[36,3,512]{2,0,1:T(8,128)} copy(f32[36,3,512]{2,0,1:T(8,128)S(1)} %bitcast.5) | data formatting | bytes 442368

commit v4 on v3

--- a/solution.py
+++ b/solution.py
@@ -52,7 +52,8 @@
     given, (wind_out, spectra_out), held = refs[:count], refs[count:count + 2], refs[count + 2:2 * count + 2]
     (wind, atm_send, spectra, sea_mask, atm_table, atm_coef, recv_cells, ocn_send, face_angle, face_ratio, slot_weight,
      send_cells, ocn_table, damping, block_count) = held
-    (ext1, ext2, rim1, rim2, surf, blk_send, blk_recv, onehot, onehot_rim, near_recv, near_send, means_own, means,
+    (ext0, names, weights, name_rim, weight_rim, name_got, weight_got, far, more_ssem, more_rsem,
+     ext1, ext2, rim1, rim2, surf, blk_send, blk_recv, onehot, onehot_rim, near_recv, near_send, means_own, means,
      trig, faces, ocn_rim, ocn_ext,
      load_sem, atm_ssem, atm_rsem, mean_ssem, mean_rsem, surf_ssem, surf_rsem, blk_ssem, blk_rsem, ocn_ssem, ocn_rsem,
      near_ssem, near_rsem) = refs[2 * count + 2:]
@@ -87,8 +88,9 @@
     for load in loads:
         load.start()
 
-    def gather_rim(ext, out):
-        tiles = [ext[:, pl.ds(rim + j * LANES, LANES)] for j in range(own_tiles)]
+    def gather_rim(ext, out, base=None):
+        base = rim if base is None else base
+        tiles = [ext[:, pl.ds(base + j * LANES, LANES)] for j in range(own_tiles)]
         for t in range(2 * rim_tiles):
             lane, high = split_index(spread8(atm_send[pl.ds(t, 1), :]))
             out[t // rim_tiles, :, pl.ds((t % rim_tiles) * LANES, LANES)] = pick(tiles, lane, high, 0)
@@ -119,18 +121,42 @@
 
         lax.fori_loop(0, own_tiles, block, 0, unroll=4)
 
-    for load in loads[:2]:
+    for load in loads:
         load.wait()
     ext1[0:levels, pl.ds(rim, cells)] = wind[0]
     ext1[levels:2 * levels, pl.ds(rim, cells)] = wind[1]
     gather_rim(ext1, rim1)
+    for side in (0, rim + cells):
+        ext0[:, pl.ds(side, rim)] = jnp.zeros((2 * levels, rim), jnp.float32)
+    ext0[0:levels, pl.ds(rim, cells)] = wind[0]
+    ext0[levels:2 * levels, pl.ds(rim, cells)] = wind[1]
+
+    def keep_once(start, here, lap):
+        ext2[:, pl.ds(rim + start, LANES)] = lap
+
+    laplace(ext0, keep_once)
+    gather_rim(ext2, rim2)
+    names[...] = jnp.zeros_like(names)
+    weights[...] = jnp.zeros_like(weights)
+    names[0:3, :] = atm_table[...]
+    weights[0:3, :] = atm_coef[...]
+    gather_rim(names, name_rim, 0)
+    gather_rim(weights, weight_rim, 0)
     pl.semaphore_wait(barrier, n_cells + n_spec - 2)
     first = rim_copies(rim1, ext1, 0)
     for copy in first:
         copy.start()
-
-    for load in loads[2:]:
-        load.wait()
+    second = rim_copies(rim2, ext2, 2)
+    more = []
+    for side, step in ((0, n_cells - 1), (1, 1)):
+        moves = ((name_rim, name_got, step), (weight_rim, weight_got, step), (rim1, far, 2 * step))
+        for q, (src, dst, by) in enumerate(moves):
+            more.append(pltpu.make_async_remote_copy(
+                src_ref=src.at[side], dst_ref=dst.at[1 - side],
+                send_sem=more_ssem.at[3 * side + q], recv_sem=more_rsem.at[3 * side + q],
+                device_id=(lax.rem(me + by, n_cells), part), device_id_type=MESH))
+    for copy in (*second, *more):
+        copy.start()
 
     def near_copies(side, other):
         at = 1 - side
@@ -173,14 +199,7 @@
     for copy in first:
         copy.wait_recv()
 
-    def keep_once(start, here, lap):
-        ext2[:, pl.ds(rim + start, LANES)] = lap
-
     laplace(ext1, keep_once)
-    gather_rim(ext2, rim2)
-    second = rim_copies(rim2, ext2, 2)
-    for copy in second:
-        copy.start()
 
     def hits(i):
         place = lax.broadcasted_iota(jnp.int32, (ocean, slots), 0)
@@ -246,8 +265,25 @@
     for copy in third:
         copy.start()
 
-    for copy in second:
+    for copy in (*second, *more):
         copy.wait_recv()
+    for side in range(2):
+        sources = (far, rim1) if side == 0 else (rim1, far)
+        for t in range(rim_tiles):
+            at = pl.ds(t * LANES, LANES)
+            spot = pl.ds(side * (rim + cells) + t * LANES, LANES)
+            total = ext2[:, spot]
+            for k in range(3):
+                lane, high = split_index(spread8(name_got[side, k:k + 1, at]))
+                low, top = (
+                    pick([source[q, :, pl.ds(j * LANES, LANES)] for j in range(rim_tiles)], lane, high, first_tile)
+                    for q, (source, first_tile) in enumerate(
+                        zip(sources, (0, rim_tiles + own_tiles)))
+                    for q in [side]
+                )
+                value = jnp.where(high < rim_tiles, low, jnp.where(high >= rim_tiles + own_tiles, top, 0.0))
+                total += spread8(weight_got[side, k:k + 1, at]) * value
+            ext2[:, spot] = total
     row = lax.broadcasted_iota(jnp.int32, (8, LANES), 0)
     rate = jnp.zeros((8, LANES), jnp.float32)
     for v in range(levels):
@@ -371,7 +407,7 @@
                     result = result - transport * jnp.where(transport > 0.0, here, upwind)
                 size = min(8, DIRECTIONS - g * 8)
                 spectra_out[k, g * 8:g * 8 + size, at] = result[0:size]
-    for copy in (*first, *second, *third, *near):
+    for copy in (*first, *second, *third, *near, *more):
         copy.wait_send()
     for step in range(1, n_spec):
         mean_copy(lax.rem(part + step, n_spec), part).wait_send()
@@ -421,6 +457,11 @@
             *(pltpu.VMEM(array.shape, array.dtype) for array in loaded[:-2]),
             *(pltpu.SMEM(array.shape, array.dtype) for array in loaded[-2:]),
             pltpu.VMEM((2 * levels, cells + 2 * rim), f32),
+            pltpu.VMEM((8, cells), jnp.int32), pltpu.VMEM((8, cells), f32),
+            pltpu.VMEM((2, 8, rim), jnp.int32), pltpu.VMEM((2, 8, rim), f32),
+            pltpu.VMEM((2, 8, rim), jnp.int32), pltpu.VMEM((2, 8, rim), f32),
+            pltpu.VMEM((2, 2 * levels, rim), f32), dma((6,)), dma((6,)),
+            pltpu.VMEM((2 * levels, cells + 2 * rim), f32),
             pltpu.VMEM((2 * levels, cells + 2 * rim), f32),
             pltpu.VMEM((2, 2 * levels, rim), f32),
             pltpu.VMEM((2, 2 * levels, rim), f32),

time: 25 us -> 25.5 us (1.020)
  Pallas kernels: 22.8 us -> 23.4 us
    pallas_call x1, Pallas kernels: 22.8 us -> 23.4 us  [local(): pl.pallas_call(functools.partial(kernel, n_cells, n_spec), out_shape=(jax...]
where the time goes in v4:
time: 25.5 us; the launch traced here: 25.4 us
  Pallas kernels  23.4 us (92%)
  local copies, waits for them, and re-layouts  1.32 us (5%)
  between operations  0.64 us (3%)
    pallas_call x1, Pallas kernels, local(): pl.pallas_call(functools.partial(kernel, n_cells, n_spec), out_shape=(jax...  23.4 us
    unnamed x2, local copies, waits for them, and re-layouts  1.32 us

profile of v4, /device:TPU:0, one launch (start us, length us, event | category | flops | bytes accessed | tf_op | source)
XLA Modules:
  0.0 25.4 jit_solution(11360760894572653323)
XLA Ops:
  0.6 23.4 %shard_map.158 = (f32[2,4,2048]{2,1,0:T(4,128)S(1)}, f32[3,36,512]{2,1,0:T(8,128)S(1)}) custom-call(f32[2,4,2048]{2,1,0:T(4,128)} %refs_0_.1, s32[8,128]{1,0:T(8,128)} %bitcast.7, f32[3,36,512]{2,1,0:T(8,128)} %bitcast.6, s32[1,512]{1,0:T(1,128)} %bitcast.8, s32[3,2048]{1,0:T(4,128)} %refs_4_.1, f32[3,2048]{1,0:T(4,128)} %refs_5_.1, s32[8,256]{1,0:T(8,128)} %refs_6_.1, ...), custom_call_target="tpu_custom_call" | custom-call | tf_op jit(solution)/shard_map/pallas_call | solution.py:448
  24.0 0.6 %copy.19 = f32[2,4,2048]{2,1,0:T(4,128)} copy(f32[2,4,2048]{2,1,0:T(4,128)S(1)} %get-tuple-element.8) | data formatting | bytes 131072
  24.7 0.7 %copy.20 = f32[36,3,512]{2,0,1:T(8,128)} copy(f32[36,3,512]{2,0,1:T(8,128)S(1)} %bitcast.5) | data formatting | bytes 442368
